TPU v7x, 256 devices: a whole 4x4x8 slice. The times are simulated.
256 devices in a mesh: gx: 16 (over y, x), gy: 16 (over z, core).
Axes of the slice: x: 4, y: 4, z: 8, core: 2. Of those that a mesh axis runs over, the one named last changes fastest.
Arguments:
- vectors: float32 [8, 128, 256, 256], P(None, 'gx', 'gy'), may hold values from -10 to 10
- weight_x: float32 [128, 256, 256], P('gx', 'gy'), may hold values from 0.05 to 1
- weight_y: float32 [128, 256, 256], P('gx', 'gy'), may hold values from 0.05 to 1
- weight_z: float32 [128, 256, 256], P('gx', 'gy'), may hold values from 0.05 to 1
Outputs:
- refined: float32 [8, 128, 256, 256], P(None, 'gx', 'gy')
- eigenvalues: float32 [8], replicated
All inputs are finite; a program needn't handle non-finite values.
Results may differ from a plain program's by a relative error of at most 0.000075.
Values sent between devices are 32-bit elements; how exact they have to be, the bound alone decides.
No kernel may reach another device: no remote copies, remote signals or barrier semaphores. Data moves between devices by JAX's collectives and lax.ppermute only.
A program may use at most 128 MiB of HBM per device.

v0:
```python
import jax
import jax.numpy as jnp
from jax import lax
from jax.sharding import PartitionSpec as P

COARSE_SWEEPS = 4
OMEGA = 0.8
SHIFT = 0.1


def shifted(shard, axis, by):
    count = lax.axis_size(axis)
    pairs = [(i, i + by) for i in range(count) if 0 <= i + by < count]
    return lax.ppermute(shard, axis, pairs)


def with_halo(cells, sides, width):
    for axis, dim in sides:
        count = lax.axis_size(axis)
        ends = count - 1
        head = lax.slice_in_dim(cells, 0, width, axis=dim)
        tail = lax.slice_in_dim(cells, cells.shape[dim] - width, cells.shape[dim], axis=dim)
        cells = jnp.concatenate(
            [
                lax.ppermute(tail, axis, [(i, (i + 1) % count) for i in range(ends)]),
                cells,
                lax.ppermute(head, axis, [((i + 1) % count, i) for i in range(ends)]),
            ],
            axis=dim,
        )
    return cells


def lower_x(weights):
    rim = shifted(weights[-1:], "gx", 1)
    return jnp.concatenate([rim, weights[:-1]], 0)


def lower_y(weights):
    rim = shifted(weights[:, -1:], "gy", 1)
    return jnp.concatenate([rim, weights[:, :-1]], 1)


def lower_z(weights):
    return jnp.concatenate([jnp.zeros_like(weights[:, :, :1]), weights[:, :, :-1]], 2)


def trimmed(array):
    return array[..., 1:-1, 1:-1, :]


def inner_sum(field, parts):
    wx, lx, wy, ly, wz, lz = parts
    centre = trimmed(field)
    zpadded = jnp.pad(centre, ((0, 0), (0, 0), (0, 0), (1, 1)))
    total = wx[None] * field[:, 2:, 1:-1] + lx[None] * field[:, :-2, 1:-1]
    total = total + wy[None] * field[:, 1:-1, 2:] + ly[None] * field[:, 1:-1, :-2]
    total = total + wz[None] * zpadded[..., 2:] + lz[None] * zpadded[..., :-2]
    return total


def neighbours(field, parts, level):
    if level == "fine":
        padded = with_halo(field, (("gx", 1), ("gy", 2)), 1)
    else:
        padded = with_halo(field, (("gx", 1), ("gy", 2)), 1)
    return inner_sum(padded, parts)


def jacobi(guess, source, diag, parts, level):
    return (
        guess
        + OMEGA * (source - (diag[None] * guess - neighbours(guess, parts, level))) / diag[None]
    )


def rayleigh_sums(vectors, applied, degree):
    return lax.psum(
        (
            jnp.sum(vectors * applied, axis=(1, 2, 3)),
            jnp.sum(vectors * (degree[None] * vectors), axis=(1, 2, 3)),
        ),
        ("gx", "gy"),
    )


def coarse_weights(wx, wy, wz, degree):
    sx, sy, sz = wx.shape
    shape = (sx // 2, 2, sy // 2, 2, sz // 2, 2)
    cx = wx.reshape(shape)[:, 1].sum(axis=(2, 4))
    cy = wy.reshape(shape)[:, :, :, 1].sum(axis=(1, 4))
    cz = wz.reshape(shape)[..., 1].sum(axis=(1, 3))
    dsum = degree.reshape(shape).sum(axis=(1, 3, 5))
    return (cx, cy, cz, dsum)


def restrict(field):
    kk, sx, sy, sz = field.shape
    return field.reshape(kk, sx // 2, 2, sy // 2, 2, sz // 2, 2).sum(axis=(2, 4, 6))


def prolong(field):
    kk, sx, sy, sz = field.shape
    return jnp.broadcast_to(field[:, :, None, :, None, :, None], (kk, sx, 2, sy, 2, sz, 2)).reshape(
        kk, 2 * sx, 2 * sy, 2 * sz
    )


def per_device(vectors, weight_x, weight_y, weight_z):
    local_x, local_y, depth = weight_x.shape
    span_x = local_x * lax.axis_size("gx")
    span_y = local_y * lax.axis_size("gy")
    pos_x = lax.axis_index("gx") * local_x + lax.broadcasted_iota(jnp.int32, (local_x, 1, 1), 0)
    pos_y = lax.axis_index("gy") * local_y + lax.broadcasted_iota(jnp.int32, (1, local_y, 1), 1)
    pos_z = lax.broadcasted_iota(jnp.int32, (1, 1, depth), 2)
    wx = jnp.where(pos_x < span_x - 1, weight_x, jnp.zeros_like(weight_x))
    wy = jnp.where(pos_y < span_y - 1, weight_y, jnp.zeros_like(weight_y))
    wz = jnp.where(pos_z < depth - 1, weight_z, jnp.zeros_like(weight_z))
    parts = (wx, lower_x(wx), wy, lower_y(wy), wz, lower_z(wz))
    degree = parts[0] + parts[1] + parts[2] + parts[3] + parts[4] + parts[5]
    applied = degree[None] * vectors - neighbours(vectors, parts, "fine")
    numer, denom = rayleigh_sums(vectors, applied, degree)
    eigenvalues = numer / denom
    resid = applied - eigenvalues[:, None, None, None] * (degree[None] * vectors)
    dfine = (1.0 + SHIFT) * degree
    guess = OMEGA * resid / dfine[None]
    guess = jacobi(guess, resid, dfine, parts, "fine")
    fine_rest = resid - (dfine[None] * guess - neighbours(guess, parts, "fine"))
    cx, cy, cz, dsum = coarse_weights(wx, wy, wz, degree)
    cparts = (cx, lower_x(cx), cy, lower_y(cy), cz, lower_z(cz))
    dcoarse = cparts[0] + cparts[1] + cparts[2] + cparts[3] + cparts[4] + cparts[5] + SHIFT * dsum
    rcoarse = restrict(fine_rest)
    correction = OMEGA * rcoarse / dcoarse[None]
    for sweep in range(COARSE_SWEEPS - 1):
        correction = jacobi(correction, rcoarse, dcoarse, cparts, "coarse")
    guess = guess + prolong(correction)
    guess = jacobi(guess, resid, dfine, parts, "fine")
    updated = vectors - guess
    local_gram = jnp.einsum(
        "aijk,bijk->ab", updated, degree[None] * updated, precision=lax.Precision.HIGHEST
    )
    gram = lax.psum(local_gram, ("gx", "gy"))
    gram = gram / (span_x * span_y * depth)
    chol = jnp.linalg.cholesky(gram)
    flat = updated.reshape(updated.shape[0], -1)
    refined = jax.scipy.linalg.solve_triangular(chol, flat, lower=True).reshape(updated.shape)
    return (refined, eigenvalues)


def solution(mesh):
    return jax.shard_map(
        per_device,
        mesh=mesh,
        in_specs=(
            P(None, "gx", "gy", None),
            P("gx", "gy", None),
            P("gx", "gy", None),
            P("gx", "gy", None),
        ),
        out_specs=(P(None, "gx", "gy", None), P()),
        check_vma=False,
    )
```

profile of v0, /device:TPU:1, one launch (start us, length us, event | category | flops | bytes accessed | tf_op | source)
XLA Modules:
  0.0 427.5 jit_solution(8508537190117706973)
XLA Ops:
  1.7 3.9 collective-permute-start
  6.6 4.4 %collective-permute-start.1 = (f32[8,1,256]{2,1,0:T(1,128)S(1)}, f32[8,1,256]{2,1,0:T(1,128)S(1)}, u32[]{:S(2)}, u32[]{:S(2)}) collective-permute-start(f32[8,1,256]{2,1,0:T(1,128)S(1)} %slice.374), channel_id=1, source_target_pairs={{0,1},{1,2},{2,3},{3,4},{4,5},{5,6},{6,7},{7,8},{8,9},{9,10},{10,1... | collective-permute-start | bytes 24584 | tf_op jit(solution)/shard_map/ppermute | solution.py:14
  12.0 3.1 collective-permute-start.3
  15.2 1.3 collective-permute-start.2
  16.5 9.8 %reshape.74 = f32[4,2,8,2,128,2]{5,4,3,2,1,0:T(8,128)} reshape(f32[8,16,256]{2,1,0:T(8,128)S(1)} %broadcast_select_fusion.2) | data formatting | bytes 262144 | tf_op jit(solution)/shard_map/reshape | solution.py:90
  26.6 1.9 collective-permute-start.4
  28.6 3.6 collective-permute-start.5
  33.8 2.1 fusion
  35.9 82.2 %all-reduce.9 = (f32[8]{0:T(128)S(1)}, f32[8]{0:T(128)S(1)}) all-reduce(f32[8]{0:T(128)S(1)} %get-tuple-element.19, f32[8]{0:T(128)S(1)} %get-tuple-element.18), channel_id=1, replica_groups=mesh['gx'=16,'gy'=16] {'gx','gy'}, use_global_device_ids=true, to_apply=%region_1.2 | all-reduce | flops 16 | bytes 128 | tf_op jit(solution)/shard_map/psum | solution.py:78
  118.1 1.7 multiply_divide_fusion
  120.6 1.3 collective-permute-start.6
  121.8 4.7 %collective-permute-start.7 = (f32[8,1,16,256]{3,2,1,0:T(8,128)}, f32[8,1,16,256]{3,2,1,0:T(8,128)}, u32[]{:S(2)}, u32[]{:S(2)}) collective-permute-start(f32[8,1,16,256]{3,2,1,0:T(8,128)} %get-tuple-element.44), channel_id=1, source_target_pairs={{0,16},{16,32},{32,48},{48,64},{64,80},{80,96},{96,112},{112,128},... | collective-permute-start | bytes 393224 | tf_op jit(solution)/shard_map/ppermute | solution.py:25
  126.5 2.8 slice_reduce_fusion.2
  130.5 2.5 collective-permute-start.14
  133.0 9.7 %reshape.75 = f32[4,2,8,2,128,2]{5,4,3,2,1,0:T(8,128)} reshape(f32[8,16,256]{2,1,0:T(8,128)S(1)} %broadcast_select_fusion.1) | data formatting | bytes 262144 | tf_op jit(solution)/shard_map/reshape | solution.py:91
  142.7 1.0 pad_maximum_fusion.62
  143.8 3.4 collective-permute-start.8
  147.2 2.9 collective-permute-start.9
  150.1 2.8 slice_reduce_fusion.1
  153.5 2.5 collective-permute-start.15
  156.1 9.8 %reshape.76 = f32[4,2,8,2,128,2]{5,4,3,2,1,0:T(8,128)} reshape(f32[8,16,256]{2,1,0:T(8,128)S(1)} %broadcast_select_fusion) | data formatting | bytes 262144 | tf_op jit(solution)/shard_map/reshape | solution.py:92
  166.1 5.3 %fusion.13 = f32[8,8,16,256]{3,2,1,0:T(8,128)S(1)} fusion(f32[8,8,16,256]{3,2,1,0:T(8,128)} %copy-done.1, f32[8,8,16,256]{3,2,1,0:T(8,128)S(1)} %get-tuple-element.27, f32[8,10,1,256]{3,2,1,0:T(1,128)S(1)} %copy.441, f32[8,1,16,256]{3,2,1,0:T(8,128)} %copy-done.25, f32[8,1,16,256]{3,2,1,0:T(8,128)} %collective-permute-done.7, ...), kind=kLoop, calls=%fused_computation.28 | loop fusion | flops 6553600 | bytes 4489216 | tf_op jit(solution)/shard_map/add | solution.py:72
  172.1 1.3 collective-permute-start.10
  173.4 4.7 %collective-permute-start.11 = (f32[8,1,16,256]{3,2,1,0:T(8,128)}, f32[8,1,16,256]{3,2,1,0:T(8,128)}, u32[]{:S(2)}, u32[]{:S(2)}) collective-permute-start(f32[8,1,16,256]{3,2,1,0:T(8,128)} %get-tuple-element.42), channel_id=1, source_target_pairs={{0,16},{16,32},{32,48},{48,64},{64,80},{80,96},{96,112},{112,128},... | collective-permute-start | bytes 393224 | tf_op jit(solution)/shard_map/ppermute | solution.py:25
  178.1 6.8 %slice_reduce_fusion = f32[4,8,128]{2,1,0:T(8,128)} fusion(f32[4,2,8,2,128,2]{5,4,3,2,1,0:T(8,128)} %reshape.76), kind=kLoop, calls=%fused_computation | loop fusion | flops 12288 | bytes 81920 | tf_op jit(solution)/shard_map/reduce_sum | solution.py:92
  184.8 10.5 %reshape.77 = f32[4,2,8,2,128,2]{5,4,3,2,1,0:T(8,128)} reshape(f32[8,16,256]{2,1,0:T(8,128)} %copy-done.8) | data formatting | bytes 262144 | tf_op jit(solution)/shard_map/reshape | solution.py:93
  195.3 4.6 %reduce_sum.69 = f32[4,8,128]{2,1,0:T(8,128)} reduce(f32[4,2,8,2,128,2]{5,4,3,2,1,0:T(8,128)} %reshape.77, f32[]{:T(128)} %constant.65.clone.1), dimensions={1,3,5}, to_apply=%region_8.9 | reduce | flops 28672 | bytes 147460 | tf_op jit(solution)/shard_map/reduce_sum | solution.py:93
  200.0 1.2 pad_maximum_fusion.59
  201.2 3.0 collective-permute-start.12
  204.3 2.5 collective-permute-start.13
  206.9 1.4 multiply_add_fusion
  208.5 2.8 fusion.19
  211.3 9.8 %copy.446 = f32[8,8,16,256]{0,3,2,1:T(8,128)} copy(f32[8,8,16,256]{3,2,1,0:T(8,128)} %fusion.19) | data formatting | bytes 2097152 | tf_op jit(solution)/shard_map/sub | solution.py:128
  221.1 13.1 %reduce_sum.65 = f32[8,4,8,128]{0,3,2,1:T(8,128)} reduce(f32[8,4,2,8,2,128,2]{0,6,5,4,3,2,1:T(2,128)} %bitcast.30, f32[]{:T(128)} %constant.65.clone.1), dimensions={2,4,6}, to_apply=%region_4.5 | reduce | flops 229376 | bytes 1179652 | tf_op jit(solution)/shard_map/reduce_sum | solution.py:99
  234.2 2.8 copy.447
  237.1 1.0 multiply_divide_fusion.1
  238.1 1.3 collective-permute-start.16
  239.4 4.0 collective-permute-start.17
  244.4 2.9 collective-permute-start.18
  247.4 4.3 %collective-permute-start.19 = (f32[8,6,1,128]{3,2,1,0:T(1,128)S(1)}, f32[8,6,1,128]{3,2,1,0:T(1,128)S(1)}, u32[]{:S(2)}, u32[]{:S(2)}) collective-permute-start(f32[8,6,1,128]{3,2,1,0:T(1,128)S(1)} %get-tuple-element.53), channel_id=1, source_target_pairs={{0,1},{1,2},{2,3},{3,4},{4,5},{5,6},{6,7},{7,8},{8,9},{9,10},{10,1... | collective-permute-start | bytes 73736 | tf_op jit(solution)/shard_map/ppermute | solution.py:25
  252.7 1.1 fusion.68
  253.8 1.3 collective-permute-start.20
  255.1 4.6 %collective-permute-start.21 = (f32[8,1,8,128]{3,2,1,0:T(8,128)S(1)}, f32[8,1,8,128]{3,2,1,0:T(8,128)S(1)}, u32[]{:S(2)}, u32[]{:S(2)}) collective-permute-start(f32[8,1,8,128]{3,2,1,0:T(8,128)S(1)} %get-tuple-element.56), channel_id=1, source_target_pairs={{0,16},{16,32},{32,48},{48,64},{64,80},{80,96},{96,112},{112,128},... | collective-permute-start | bytes 98312 | tf_op jit(solution)/shard_map/ppermute | solution.py:25
  260.7 1.9 collective-permute-start.22
  262.6 5.1 %collective-permute-start.23 = (f32[8,6,1,128]{3,2,1,0:T(1,128)S(1)}, f32[8,6,1,128]{3,2,1,0:T(1,128)S(1)}, u32[]{:S(2)}, u32[]{:S(2)}) collective-permute-start(f32[8,6,1,128]{3,2,1,0:T(1,128)S(1)} %get-tuple-element.51), channel_id=1, source_target_pairs={{0,1},{1,2},{2,3},{3,4},{4,5},{5,6},{6,7},{7,8},{8,9},{9,10},{10,1... | collective-permute-start | bytes 73736 | tf_op jit(solution)/shard_map/ppermute | solution.py:25
  268.8 1.3 collective-permute-start.24
  270.1 4.6 %collective-permute-start.25 = (f32[8,1,8,128]{3,2,1,0:T(8,128)S(1)}, f32[8,1,8,128]{3,2,1,0:T(8,128)S(1)}, u32[]{:S(2)}, u32[]{:S(2)}) collective-permute-start(f32[8,1,8,128]{3,2,1,0:T(8,128)S(1)} %get-tuple-element.54), channel_id=1, source_target_pairs={{0,16},{16,32},{32,48},{48,64},{64,80},{80,96},{96,112},{112,128},... | collective-permute-start | bytes 98312 | tf_op jit(solution)/shard_map/ppermute | solution.py:25
  275.8 1.9 collective-permute-start.26
  277.7 5.1 %collective-permute-start.27 = (f32[8,6,1,128]{3,2,1,0:T(1,128)S(1)}, f32[8,6,1,128]{3,2,1,0:T(1,128)S(1)}, u32[]{:S(2)}, u32[]{:S(2)}) collective-permute-start(f32[8,6,1,128]{3,2,1,0:T(1,128)S(1)} %get-tuple-element.49), channel_id=1, source_target_pairs={{0,1},{1,2},{2,3},{3,4},{4,5},{5,6},{6,7},{7,8},{8,9},{9,10},{10,1... | collective-permute-start | bytes 73736 | tf_op jit(solution)/shard_map/ppermute | solution.py:25
  284.5 2.9 copy.451
  287.4 7.1 %broadcast_in_dim.30 = f32[8,4,2,8,2,128,2]{0,6,5,4,3,2,1:T(2,128)} broadcast(f32[8,4,8,128]{0,3,2,1:T(8,128)} %copy.451), dimensions={0,1,3,5} | broadcast | bytes 1179648 | tf_op jit(solution)/shard_map/broadcast_in_dim | solution.py:104
  294.5 10.6 %copy.452 = f32[8,8,16,256]{3,2,1,0:T(8,128)} copy(f32[8,8,16,256]{0,3,2,1:T(8,128)} %bitcast.31) | data formatting | bytes 2097152 | tf_op jit(solution)/shard_map/reshape | solution.py:104
  305.1 1.4 add.263
  306.6 1.4 collective-permute-start.28
  308.1 4.6 %collective-permute-start.29 = (f32[8,1,16,256]{3,2,1,0:T(8,128)S(1)}, f32[8,1,16,256]{3,2,1,0:T(8,128)S(1)}, u32[]{:S(2)}, u32[]{:S(2)}) collective-permute-start(f32[8,1,16,256]{3,2,1,0:T(8,128)S(1)} %get-tuple-element.40), channel_id=1, source_target_pairs={{0,16},{16,32},{32,48},{48,64},{64,80},{80,96},{96,112},{112,128},... | collective-permute-start | bytes 393224 | tf_op jit(solution)/shard_map/ppermute | solution.py:25
  313.1 1.5 collective-permute-done.29
  314.7 1.9 collective-permute-start.30
  316.7 5.3 %collective-permute-start.31 = (f32[8,10,1,256]{3,0,2,1:T(8,128)S(1)}, f32[8,10,1,256]{3,0,2,1:T(8,128)S(1)}, u32[]{:S(2)}, u32[]{:S(2)}) collective-permute-start(f32[8,10,1,256]{3,0,2,1:T(8,128)S(1)} %copy.455), channel_id=1, source_target_pairs={{0,1},{1,2},{2,3},{3,4},{4,5},{5,6},{6,7},{7,8},{8,9},{9,10},{10,1... | collective-permute-start | bytes 245768 | tf_op jit(solution)/shard_map/ppermute | solution.py:25
  322.1 1.1 collective-permute-done.31
  323.3 1.6 broadcast_multiply_fusion
  324.9 3.0 convolution_bitcast_fusion
  327.9 93.9 %psum.23 = f32[8,8]{0,1:T(8,128)S(1)} all-reduce(f32[8,8]{0,1:T(8,128)S(1)} %convolution_bitcast_fusion), channel_id=1, replica_groups=mesh['gx'=16,'gy'=16] {'gx','gy'}, use_global_device_ids=true, to_apply=%region_9.10 | all-reduce | flops 64 | bytes 512 | tf_op jit(solution)/shard_map/psum | solution.py:142
  425.1 1.0 fusion.110
  426.2 1.3 copy.462
  (158 shorter events, 19.4 us)
Async XLA Ops:
  1.6 24.6 %copy-start.2 = (f32[8,16,256]{2,1,0:T(8,128)}, f32[8,16,256]{2,1,0:T(8,128)S(1)}, u32[]{:S(2)}) copy-start(f32[8,16,256]{2,1,0:T(8,128)S(1)} %broadcast_select_fusion.2) | copy-start | bytes 393220
  1.7 30.6 %collective-permute-start = (f32[1,16,256]{2,1,0:T(8,128)S(1)}, f32[1,16,256]{2,1,0:T(8,128)S(1)}, u32[]{:S(2)}, u32[]{:S(2)}) collective-permute-start(f32[1,16,256]{2,1,0:T(8,128)S(1)} %slice.372), channel_id=1, source_target_pairs={{0,16},{16,32},{32,48},{48,64},{64,80},{80,96},{96,112},{112,128},... | collective-permute-start | bytes 49160 | tf_op jit(solution)/shard_map/ppermute | solution.py:14
  6.6 25.6 %collective-permute-start.1 = (f32[8,1,256]{2,1,0:T(1,128)S(1)}, f32[8,1,256]{2,1,0:T(1,128)S(1)}, u32[]{:S(2)}, u32[]{:S(2)}) collective-permute-start(f32[8,1,256]{2,1,0:T(1,128)S(1)} %slice.374), channel_id=1, source_target_pairs={{0,1},{1,2},{2,3},{3,4},{4,5},{5,6},{6,7},{7,8},{8,9},{9,10},{10,1... | collective-permute-start | bytes 24584 | tf_op jit(solution)/shard_map/ppermute | solution.py:14
  12.0 14.3 %collective-permute-start.3 = (f32[8,1,16,256]{3,2,1,0:T(8,128)S(1)}, f32[8,1,16,256]{3,2,1,0:T(8,128)S(1)}, u32[]{:S(2)}, u32[]{:S(2)}) collective-permute-start(f32[8,1,16,256]{3,2,1,0:T(8,128)S(1)} %get-tuple-element.47), channel_id=1, source_target_pairs={{0,16},{16,32},{32,48},{48,64},{64,80},{80,96},{96,112},{112,128},... | collective-permute-start | bytes 393224 | tf_op jit(solution)/shard_map/ppermute | solution.py:25
  15.2 11.3 %collective-permute-start.2 = (f32[8,1,16,256]{3,2,1,0:T(8,128)S(1)}, f32[8,1,16,256]{3,2,1,0:T(8,128)S(1)}, u32[]{:S(2)}, u32[]{:S(2)}) collective-permute-start(f32[8,1,16,256]{3,2,1,0:T(8,128)S(1)} %get-tuple-element.46), channel_id=1, source_target_pairs={{16,0},{32,16},{48,32},{64,48},{80,64},{96,80},{112,96},{128,112},... | collective-permute-start | bytes 393224 | tf_op jit(solution)/shard_map/ppermute | solution.py:27
  16.5 9.8 %copy-start.26 = (f32[8,16,256]{2,1,0:T(8,128)S(1)}, f32[8,16,256]{2,1,0:T(8,128)}, u32[]{:S(2)}) copy-start(f32[8,16,256]{2,1,0:T(8,128)} %param.7) | copy-start | bytes 393220
  16.5 9.8 %copy-start = (f32[8,8,16,256]{3,2,1,0:T(8,128)S(1)}, f32[8,8,16,256]{3,2,1,0:T(8,128)}, u32[]{:S(2)}) copy-start(f32[8,8,16,256]{3,2,1,0:T(8,128)} %param.4) | copy-start | bytes 3145732
  26.3 5.9 %slice-start = ((f32[8,16,256]{2,1,0:T(8,128)}), f32[7,16,256]{2,1,0:T(8,128)S(1)}, s32[]{:S(2)}) async-start(f32[8,16,256]{2,1,0:T(8,128)} %copy-done.2), calls=%async_computation | async-start | bytes 229376 | tf_op jit(solution)/shard_map/slice | solution.py:36
  26.3 5.9 %copy-start.27 = (f32[8,16,256]{2,1,0:T(8,128)S(1)}, f32[8,16,256]{2,1,0:T(8,128)}, u32[]{:S(2)}) copy-start(f32[8,16,256]{2,1,0:T(8,128)} %param.5) | copy-start | bytes 393220
  26.3 5.9 %copy-start.28 = (f32[8,16,256]{2,1,0:T(8,128)S(1)}, f32[8,16,256]{2,1,0:T(8,128)}, u32[]{:S(2)}) copy-start(f32[8,16,256]{2,1,0:T(8,128)} %param.6) | copy-start | bytes 393220
  26.5 7.3 %copy-start.3 = (f32[8,16,256]{2,1,0:T(8,128)S(1)}, f32[8,16,256]{2,1,0:T(8,128)}, u32[]{:S(2)}) copy-start(f32[8,16,256]{2,1,0:T(8,128)} %copy-done.2) | copy-start | bytes 393220
  26.6 6.4 %collective-permute-start.4 = (f32[8,10,1,256]{3,0,2,1:T(8,128)S(1)}, f32[8,10,1,256]{3,0,2,1:T(8,128)S(1)}, u32[]{:S(2)}, u32[]{:S(2)}) collective-permute-start(f32[8,10,1,256]{3,0,2,1:T(8,128)S(1)} %copy.466), channel_id=1, source_target_pairs={{1,0},{2,1},{3,2},{4,3},{5,4},{6,5},{7,6},{8,7},{9,8},{10,9},{11,1... | collective-permute-start | bytes 245768 | tf_op jit(solution)/shard_map/ppermute | solution.py:27
  28.6 5.1 %collective-permute-start.5 = (f32[8,10,1,256]{3,0,2,1:T(8,128)S(1)}, f32[8,10,1,256]{3,0,2,1:T(8,128)S(1)}, u32[]{:S(2)}, u32[]{:S(2)}) collective-permute-start(f32[8,10,1,256]{3,0,2,1:T(8,128)S(1)} %copy.467), channel_id=1, source_target_pairs={{0,1},{1,2},{2,3},{3,4},{4,5},{5,6},{6,7},{7,8},{8,9},{9,10},{10,1... | collective-permute-start | bytes 245768 | tf_op jit(solution)/shard_map/ppermute | solution.py:25
  33.1 2.8 copy-start.17
  33.8 84.3 %copy-start.5 = (f32[8,16,256]{2,1,0:T(8,128)S(1)}, f32[8,16,256]{2,1,0:T(8,128)}, u32[]{:S(2)}) copy-start(f32[8,16,256]{2,1,0:T(8,128)} %get-tuple-element.28) | copy-start | bytes 393220
  119.8 22.9 %copy-start.1 = (f32[8,8,16,256]{3,2,1,0:T(8,128)}, f32[8,8,16,256]{3,2,1,0:T(8,128)S(1)}, u32[]{:S(2)}) copy-start(f32[8,8,16,256]{3,2,1,0:T(8,128)S(1)} %get-tuple-element.26) | copy-start | bytes 3145732
  120.6 22.2 %collective-permute-start.6 = (f32[8,1,16,256]{3,2,1,0:T(8,128)}, f32[8,1,16,256]{3,2,1,0:T(8,128)S(1)}, u32[]{:S(2)}, u32[]{:S(2)}) collective-permute-start(f32[8,1,16,256]{3,2,1,0:T(8,128)} %get-tuple-element.45), channel_id=1, source_target_pairs={{16,0},{32,16},{48,32},{64,48},{80,64},{96,80},{112,96},{128,112},... | collective-permute-start | bytes 393224 | tf_op jit(solution)/shard_map/ppermute | solution.py:27
  121.8 20.9 %collective-permute-start.7 = (f32[8,1,16,256]{3,2,1,0:T(8,128)}, f32[8,1,16,256]{3,2,1,0:T(8,128)}, u32[]{:S(2)}, u32[]{:S(2)}) collective-permute-start(f32[8,1,16,256]{3,2,1,0:T(8,128)} %get-tuple-element.44), channel_id=1, source_target_pairs={{0,16},{16,32},{32,48},{48,64},{64,80},{80,96},{96,112},{112,128},... | collective-permute-start | bytes 393224 | tf_op jit(solution)/shard_map/ppermute | solution.py:25
  130.5 76.3 %collective-permute-start.14 = (f32[1,8,128]{2,1,0:T(8,128)}, f32[1,8,128]{2,1,0:T(8,128)}, u32[]{:S(2)}, u32[]{:S(2)}) collective-permute-start(f32[1,8,128]{2,1,0:T(8,128)} %slice.384), channel_id=1, source_target_pairs={{0,16},{16,32},{32,48},{48,64},{64,80},{80,96},{96,112},{112,128},... | collective-permute-start | bytes 12296 | tf_op jit(solution)/shard_map/ppermute | solution.py:14
  142.7 10.2 %copy-start.25 = (f32[8,1,16,256]{3,2,1,0:T(8,128)}, f32[8,1,16,256]{3,2,1,0:T(8,128)S(1)}, u32[]{:S(2)}) copy-start(f32[8,1,16,256]{3,2,1,0:T(8,128)S(1)} %collective-permute-done.6) | copy-start | bytes 393220
  143.8 22.1 %collective-permute-start.8 = (f32[8,10,1,256]{3,0,2,1:T(8,128)S(1)}, f32[8,10,1,256]{3,0,2,1:T(8,128)S(1)}, u32[]{:S(2)}, u32[]{:S(2)}) collective-permute-start(f32[8,10,1,256]{3,0,2,1:T(8,128)S(1)} %copy.438), channel_id=1, source_target_pairs={{1,0},{2,1},{3,2},{4,3},{5,4},{6,5},{7,6},{8,7},{9,8},{10,9},{11,1... | collective-permute-start | bytes 245768 | tf_op jit(solution)/shard_map/ppermute | solution.py:27
  147.2 18.7 %collective-permute-start.9 = (f32[8,10,1,256]{3,0,2,1:T(8,128)S(1)}, f32[8,10,1,256]{3,0,2,1:T(8,128)S(1)}, u32[]{:S(2)}, u32[]{:S(2)}) collective-permute-start(f32[8,10,1,256]{3,0,2,1:T(8,128)S(1)} %copy.440), channel_id=1, source_target_pairs={{0,1},{1,2},{2,3},{3,4},{4,5},{5,6},{6,7},{7,8},{8,9},{9,10},{10,1... | collective-permute-start | bytes 245768 | tf_op jit(solution)/shard_map/ppermute | solution.py:25
  153.5 12.5 %copy-start.4 = (f32[8,16,256]{2,1,0:T(8,128)S(1)}, f32[8,16,256]{2,1,0:T(8,128)}, u32[]{:S(2)}) copy-start(f32[8,16,256]{2,1,0:T(8,128)} %copy-done.2) | copy-start | bytes 393220
  153.5 53.3 %collective-permute-start.15 = (f32[4,1,128]{2,1,0:T(1,128)}, f32[4,1,128]{2,1,0:T(1,128)}, u32[]{:S(2)}, u32[]{:S(2)}) collective-permute-start(f32[4,1,128]{2,1,0:T(1,128)} %slice.387), channel_id=1, source_target_pairs={{0,1},{1,2},{2,3},{3,4},{4,5},{5,6},{6,7},{7,8},{8,9},{9,10},{10,1... | collective-permute-start | bytes 6152 | tf_op jit(solution)/shard_map/ppermute | solution.py:14
  172.1 27.9 %collective-permute-start.10 = (f32[8,1,16,256]{3,2,1,0:T(8,128)}, f32[8,1,16,256]{3,2,1,0:T(8,128)}, u32[]{:S(2)}, u32[]{:S(2)}) collective-permute-start(f32[8,1,16,256]{3,2,1,0:T(8,128)} %get-tuple-element.43), channel_id=1, source_target_pairs={{16,0},{32,16},{48,32},{64,48},{80,64},{96,80},{112,96},{128,112},... | collective-permute-start | bytes 393224 | tf_op jit(solution)/shard_map/ppermute | solution.py:27
  173.4 26.6 %collective-permute-start.11 = (f32[8,1,16,256]{3,2,1,0:T(8,128)}, f32[8,1,16,256]{3,2,1,0:T(8,128)}, u32[]{:S(2)}, u32[]{:S(2)}) collective-permute-start(f32[8,1,16,256]{3,2,1,0:T(8,128)} %get-tuple-element.42), channel_id=1, source_target_pairs={{0,16},{16,32},{32,48},{48,64},{64,80},{80,96},{96,112},{112,128},... | collective-permute-start | bytes 393224 | tf_op jit(solution)/shard_map/ppermute | solution.py:25
  200.0 6.9 %copy-start.21 = (f32[4,8,128]{2,1,0:T(8,128)S(1)}, f32[4,8,128]{2,1,0:T(8,128)}, u32[]{:S(2)}) copy-start(f32[4,8,128]{2,1,0:T(8,128)} %copy-done.20) | copy-start | bytes 49156
  200.0 6.9 %slice-start.1 = ((f32[4,8,128]{2,1,0:T(8,128)}), f32[3,8,128]{2,1,0:T(8,128)S(1)}, s32[]{:S(2)}) async-start(f32[4,8,128]{2,1,0:T(8,128)} %copy-done.20), calls=%async_computation.1 | async-start | bytes 24576 | tf_op jit(solution)/shard_map/slice | solution.py:36
  200.0 6.9 %copy-start.23 = (f32[4,8,128]{2,1,0:T(8,128)S(1)}, f32[4,8,128]{2,1,0:T(8,128)}, u32[]{:S(2)}) copy-start(f32[4,8,128]{2,1,0:T(8,128)} %slice_reduce_fusion) | copy-start | bytes 49156
  200.0 6.9 %copy-start.33 = (f32[4,8,128]{2,1,0:T(8,128)S(1)}, f32[4,8,128]{2,1,0:T(8,128)}, u32[]{:S(2)}) copy-start(f32[4,8,128]{2,1,0:T(8,128)} %reduce_sum.69) | copy-start | bytes 49156
  200.0 8.5 %copy-start.6 = (f32[8,16,256]{2,1,0:T(8,128)S(1)}, f32[8,16,256]{2,1,0:T(8,128)}, u32[]{:S(2)}) copy-start(f32[8,16,256]{2,1,0:T(8,128)} %get-tuple-element.28) | copy-start | bytes 393220
  200.0 8.5 %copy-start.12 = (f32[8,16,256]{2,1,0:T(8,128)S(1)}, f32[8,16,256]{2,1,0:T(8,128)}, u32[]{:S(2)}) copy-start(f32[8,16,256]{2,1,0:T(8,128)} %copy-done.11) | copy-start | bytes 393220
  200.0 8.5 %copy-start.15 = (f32[8,16,256]{2,1,0:T(8,128)S(1)}, f32[8,16,256]{2,1,0:T(8,128)}, u32[]{:S(2)}) copy-start(f32[8,16,256]{2,1,0:T(8,128)} %copy-done.14) | copy-start | bytes 393220
  200.0 8.5 %copy-start.18 = (f32[8,16,256]{2,1,0:T(8,128)S(1)}, f32[8,16,256]{2,1,0:T(8,128)}, u32[]{:S(2)}) copy-start(f32[8,16,256]{2,1,0:T(8,128)} %copy-done.17) | copy-start | bytes 393220
  201.2 7.0 %collective-permute-start.12 = (f32[8,10,1,256]{3,0,2,1:T(8,128)S(1)}, f32[8,10,1,256]{3,0,2,1:T(8,128)S(1)}, u32[]{:S(2)}, u32[]{:S(2)}) collective-permute-start(f32[8,10,1,256]{3,0,2,1:T(8,128)S(1)} %copy.442), channel_id=1, source_target_pairs={{1,0},{2,1},{3,2},{4,3},{5,4},{6,5},{7,6},{8,7},{9,8},{10,9},{11,1... | collective-permute-start | bytes 245768 | tf_op jit(solution)/shard_map/ppermute | solution.py:27
  204.3 4.1 collective-permute-start.13
  237.0 31.6 %copy-start.10 = (f32[8,4,8,128]{3,2,1,0:T(8,128)S(1)}, f32[8,4,8,128]{3,2,1,0:T(8,128)}, u32[]{:S(2)}) copy-start(f32[8,4,8,128]{3,2,1,0:T(8,128)} %copy.447) | copy-start | bytes 393220
  237.0 31.6 %copy-start.22 = (f32[4,8,128]{2,1,0:T(8,128)S(1)}, f32[4,8,128]{2,1,0:T(8,128)}, u32[]{:S(2)}) copy-start(f32[4,8,128]{2,1,0:T(8,128)} %copy-done.20) | copy-start | bytes 49156
  237.0 31.6 %copy-start.24 = (f32[4,8,128]{2,1,0:T(8,128)S(1)}, f32[4,8,128]{2,1,0:T(8,128)}, u32[]{:S(2)}) copy-start(f32[4,8,128]{2,1,0:T(8,128)} %slice_reduce_fusion) | copy-start | bytes 49156
  237.0 31.6 %copy-start.29 = (f32[4,8,128]{2,1,0:T(8,128)S(1)}, f32[4,8,128]{2,1,0:T(8,128)}, u32[]{:S(2)}) copy-start(f32[4,8,128]{2,1,0:T(8,128)} %get-tuple-element.24) | copy-start | bytes 49156
  237.0 31.6 %copy-start.30 = (f32[4,8,128]{2,1,0:T(8,128)S(1)}, f32[4,8,128]{2,1,0:T(8,128)}, u32[]{:S(2)}) copy-start(f32[4,8,128]{2,1,0:T(8,128)} %get-tuple-element.25) | copy-start | bytes 49156
  237.0 31.6 %copy-start.31 = (f32[4,8,128]{2,1,0:T(8,128)S(1)}, f32[4,8,128]{2,1,0:T(8,128)}, u32[]{:S(2)}) copy-start(f32[4,8,128]{2,1,0:T(8,128)} %get-tuple-element.62) | copy-start | bytes 49156
  237.1 31.6 %copy-start.32 = (f32[4,8,128]{2,1,0:T(8,128)S(1)}, f32[4,8,128]{2,1,0:T(8,128)}, u32[]{:S(2)}) copy-start(f32[4,8,128]{2,1,0:T(8,128)} %get-tuple-element.63) | copy-start | bytes 49156
  238.1 5.3 %collective-permute-start.16 = (f32[8,1,8,128]{3,2,1,0:T(8,128)S(1)}, f32[8,1,8,128]{3,2,1,0:T(8,128)S(1)}, u32[]{:S(2)}, u32[]{:S(2)}) collective-permute-start(f32[8,1,8,128]{3,2,1,0:T(8,128)S(1)} %get-tuple-element.59), channel_id=1, source_target_pairs={{16,0},{32,16},{48,32},{64,48},{80,64},{96,80},{112,96},{128,112},... | collective-permute-start | bytes 98312 | tf_op jit(solution)/shard_map/ppermute | solution.py:27
  239.4 5.0 %collective-permute-start.17 = (f32[8,1,8,128]{3,2,1,0:T(8,128)S(1)}, f32[8,1,8,128]{3,2,1,0:T(8,128)S(1)}, u32[]{:S(2)}, u32[]{:S(2)}) collective-permute-start(f32[8,1,8,128]{3,2,1,0:T(8,128)S(1)} %get-tuple-element.58), channel_id=1, source_target_pairs={{0,16},{16,32},{32,48},{48,64},{64,80},{80,96},{96,112},{112,128},... | collective-permute-start | bytes 98312 | tf_op jit(solution)/shard_map/ppermute | solution.py:25
  244.4 7.3 %collective-permute-start.18 = (f32[8,6,1,128]{3,2,1,0:T(1,128)S(1)}, f32[8,6,1,128]{3,2,1,0:T(1,128)S(1)}, u32[]{:S(2)}, u32[]{:S(2)}) collective-permute-start(f32[8,6,1,128]{3,2,1,0:T(1,128)S(1)} %get-tuple-element.52), channel_id=1, source_target_pairs={{1,0},{2,1},{3,2},{4,3},{5,4},{6,5},{7,6},{8,7},{9,8},{10,9},{11,1... | collective-permute-start | bytes 73736 | tf_op jit(solution)/shard_map/ppermute | solution.py:27
  247.4 5.3 %collective-permute-start.19 = (f32[8,6,1,128]{3,2,1,0:T(1,128)S(1)}, f32[8,6,1,128]{3,2,1,0:T(1,128)S(1)}, u32[]{:S(2)}, u32[]{:S(2)}) collective-permute-start(f32[8,6,1,128]{3,2,1,0:T(1,128)S(1)} %get-tuple-element.53), channel_id=1, source_target_pairs={{0,1},{1,2},{2,3},{3,4},{4,5},{5,6},{6,7},{7,8},{8,9},{9,10},{10,1... | collective-permute-start | bytes 73736 | tf_op jit(solution)/shard_map/ppermute | solution.py:25
  253.8 5.9 %collective-permute-start.20 = (f32[8,1,8,128]{3,2,1,0:T(8,128)S(1)}, f32[8,1,8,128]{3,2,1,0:T(8,128)S(1)}, u32[]{:S(2)}, u32[]{:S(2)}) collective-permute-start(f32[8,1,8,128]{3,2,1,0:T(8,128)S(1)} %get-tuple-element.57), channel_id=1, source_target_pairs={{16,0},{32,16},{48,32},{64,48},{80,64},{96,80},{112,96},{128,112},... | collective-permute-start | bytes 98312 | tf_op jit(solution)/shard_map/ppermute | solution.py:27
  255.1 5.6 %collective-permute-start.21 = (f32[8,1,8,128]{3,2,1,0:T(8,128)S(1)}, f32[8,1,8,128]{3,2,1,0:T(8,128)S(1)}, u32[]{:S(2)}, u32[]{:S(2)}) collective-permute-start(f32[8,1,8,128]{3,2,1,0:T(8,128)S(1)} %get-tuple-element.56), channel_id=1, source_target_pairs={{0,16},{16,32},{32,48},{48,64},{64,80},{80,96},{96,112},{112,128},... | collective-permute-start | bytes 98312 | tf_op jit(solution)/shard_map/ppermute | solution.py:25
  260.7 7.0 %collective-permute-start.22 = (f32[8,6,1,128]{3,2,1,0:T(1,128)S(1)}, f32[8,6,1,128]{3,2,1,0:T(1,128)S(1)}, u32[]{:S(2)}, u32[]{:S(2)}) collective-permute-start(f32[8,6,1,128]{3,2,1,0:T(1,128)S(1)} %get-tuple-element.50), channel_id=1, source_target_pairs={{1,0},{2,1},{3,2},{4,3},{5,4},{6,5},{7,6},{8,7},{9,8},{10,9},{11,1... | collective-permute-start | bytes 73736 | tf_op jit(solution)/shard_map/ppermute | solution.py:27
  262.6 6.0 %collective-permute-start.23 = (f32[8,6,1,128]{3,2,1,0:T(1,128)S(1)}, f32[8,6,1,128]{3,2,1,0:T(1,128)S(1)}, u32[]{:S(2)}, u32[]{:S(2)}) collective-permute-start(f32[8,6,1,128]{3,2,1,0:T(1,128)S(1)} %get-tuple-element.51), channel_id=1, source_target_pairs={{0,1},{1,2},{2,3},{3,4},{4,5},{5,6},{6,7},{7,8},{8,9},{9,10},{10,1... | collective-permute-start | bytes 73736 | tf_op jit(solution)/shard_map/ppermute | solution.py:25
  268.8 5.9 %collective-permute-start.24 = (f32[8,1,8,128]{3,2,1,0:T(8,128)S(1)}, f32[8,1,8,128]{3,2,1,0:T(8,128)S(1)}, u32[]{:S(2)}, u32[]{:S(2)}) collective-permute-start(f32[8,1,8,128]{3,2,1,0:T(8,128)S(1)} %get-tuple-element.55), channel_id=1, source_target_pairs={{16,0},{32,16},{48,32},{64,48},{80,64},{96,80},{112,96},{128,112},... | collective-permute-start | bytes 98312 | tf_op jit(solution)/shard_map/ppermute | solution.py:27
  270.1 5.6 %collective-permute-start.25 = (f32[8,1,8,128]{3,2,1,0:T(8,128)S(1)}, f32[8,1,8,128]{3,2,1,0:T(8,128)S(1)}, u32[]{:S(2)}, u32[]{:S(2)}) collective-permute-start(f32[8,1,8,128]{3,2,1,0:T(8,128)S(1)} %get-tuple-element.54), channel_id=1, source_target_pairs={{0,16},{16,32},{32,48},{48,64},{64,80},{80,96},{96,112},{112,128},... | collective-permute-start | bytes 98312 | tf_op jit(solution)/shard_map/ppermute | solution.py:25
  275.8 7.0 %collective-permute-start.26 = (f32[8,6,1,128]{3,2,1,0:T(1,128)S(1)}, f32[8,6,1,128]{3,2,1,0:T(1,128)S(1)}, u32[]{:S(2)}, u32[]{:S(2)}) collective-permute-start(f32[8,6,1,128]{3,2,1,0:T(1,128)S(1)} %get-tuple-element.48), channel_id=1, source_target_pairs={{1,0},{2,1},{3,2},{4,3},{5,4},{6,5},{7,6},{8,7},{9,8},{10,9},{11,1... | collective-permute-start | bytes 73736 | tf_op jit(solution)/shard_map/ppermute | solution.py:27
  277.7 6.0 %collective-permute-start.27 = (f32[8,6,1,128]{3,2,1,0:T(1,128)S(1)}, f32[8,6,1,128]{3,2,1,0:T(1,128)S(1)}, u32[]{:S(2)}, u32[]{:S(2)}) collective-permute-start(f32[8,6,1,128]{3,2,1,0:T(1,128)S(1)} %get-tuple-element.49), channel_id=1, source_target_pairs={{0,1},{1,2},{2,3},{3,4},{4,5},{5,6},{6,7},{7,8},{8,9},{9,10},{10,1... | collective-permute-start | bytes 73736 | tf_op jit(solution)/shard_map/ppermute | solution.py:25
  306.5 16.7 %copy-start.7 = (f32[8,16,256]{2,1,0:T(8,128)S(1)}, f32[8,16,256]{2,1,0:T(8,128)}, u32[]{:S(2)}) copy-start(f32[8,16,256]{2,1,0:T(8,128)} %get-tuple-element.28) | copy-start | bytes 393220
  306.6 16.7 %copy-start.9 = (f32[8,16,256]{2,1,0:T(8,128)S(1)}, f32[8,16,256]{2,1,0:T(8,128)}, u32[]{:S(2)}) copy-start(f32[8,16,256]{2,1,0:T(8,128)} %copy-done.8) | copy-start | bytes 393220
  306.6 16.7 %copy-start.13 = (f32[8,16,256]{2,1,0:T(8,128)S(1)}, f32[8,16,256]{2,1,0:T(8,128)}, u32[]{:S(2)}) copy-start(f32[8,16,256]{2,1,0:T(8,128)} %copy-done.11) | copy-start | bytes 393220
  306.6 16.7 %copy-start.16 = (f32[8,16,256]{2,1,0:T(8,128)S(1)}, f32[8,16,256]{2,1,0:T(8,128)}, u32[]{:S(2)}) copy-start(f32[8,16,256]{2,1,0:T(8,128)} %copy-done.14) | copy-start | bytes 393220
  306.6 16.7 %copy-start.19 = (f32[8,16,256]{2,1,0:T(8,128)S(1)}, f32[8,16,256]{2,1,0:T(8,128)}, u32[]{:S(2)}) copy-start(f32[8,16,256]{2,1,0:T(8,128)} %copy-done.17) | copy-start | bytes 393220
  306.6 6.5 %collective-permute-start.28 = (f32[8,1,16,256]{3,2,1,0:T(8,128)S(1)}, f32[8,1,16,256]{3,2,1,0:T(8,128)S(1)}, u32[]{:S(2)}, u32[]{:S(2)}) collective-permute-start(f32[8,1,16,256]{3,2,1,0:T(8,128)S(1)} %get-tuple-element.41), channel_id=1, source_target_pairs={{16,0},{32,16},{48,32},{64,48},{80,64},{96,80},{112,96},{128,112},... | collective-permute-start | bytes 393224 | tf_op jit(solution)/shard_map/ppermute | solution.py:27
  308.1 6.5 %collective-permute-start.29 = (f32[8,1,16,256]{3,2,1,0:T(8,128)S(1)}, f32[8,1,16,256]{3,2,1,0:T(8,128)S(1)}, u32[]{:S(2)}, u32[]{:S(2)}) collective-permute-start(f32[8,1,16,256]{3,2,1,0:T(8,128)S(1)} %get-tuple-element.40), channel_id=1, source_target_pairs={{0,16},{16,32},{32,48},{48,64},{64,80},{80,96},{96,112},{112,128},... | collective-permute-start | bytes 393224 | tf_op jit(solution)/shard_map/ppermute | solution.py:25
  314.7 7.2 %collective-permute-start.30 = (f32[8,10,1,256]{3,0,2,1:T(8,128)S(1)}, f32[8,10,1,256]{3,0,2,1:T(8,128)S(1)}, u32[]{:S(2)}, u32[]{:S(2)}) collective-permute-start(f32[8,10,1,256]{3,0,2,1:T(8,128)S(1)} %copy.453), channel_id=1, source_target_pairs={{1,0},{2,1},{3,2},{4,3},{5,4},{6,5},{7,6},{8,7},{9,8},{10,9},{11,1... | collective-permute-start | bytes 245768 | tf_op jit(solution)/shard_map/ppermute | solution.py:27
  316.7 6.5 %collective-permute-start.31 = (f32[8,10,1,256]{3,0,2,1:T(8,128)S(1)}, f32[8,10,1,256]{3,0,2,1:T(8,128)S(1)}, u32[]{:S(2)}, u32[]{:S(2)}) collective-permute-start(f32[8,10,1,256]{3,0,2,1:T(8,128)S(1)} %copy.455), channel_id=1, source_target_pairs={{0,1},{1,2},{2,3},{3,4},{4,5},{5,6},{6,7},{7,8},{8,9},{9,10},{10,1... | collective-permute-start | bytes 245768 | tf_op jit(solution)/shard_map/ppermute | solution.py:25
  (5 other events, 10.8 us)
where the time goes:
time: 429 us; the launch traced here: 427 us
  blocking collectives  176 us (41%)
  starting transfers between devices  98.6 us (23%)
  local copies, waits for them, and re-layouts  80.4 us (19%)
  other arithmetic  57.3 us (13%)
  waiting for transfers between devices  9.35 us (2%)
    psum x1, blocking collectives, per_device(): gram = lax.psum(local_gram, ('gx', 'gy'))  93.9 us
    psum x1, blocking collectives, rayleigh_sums(): lax.psum((jnp.sum(vectors * applied, axis=(1, 2, 3)), jnp.sum(vectors * (...  82.2 us
    ppermute x14, starting transfers between devices, with_halo(): lax.ppermute(tail, axis, [(i, (i + 1) % count) for i in range(ends)])  59 us
    ppermute x14, starting transfers between devices, with_halo(): lax.ppermute(head, axis, [((i + 1) % count, i) for i in range(ends)])  26.2 us
    ppermute x4, starting transfers between devices, shifted(): return lax.ppermute(shard, axis, pairs)  13.3 us
    reduce_sum x1, other arithmetic, restrict(): field.reshape(kk, sx // 2, 2, sy // 2, 2, sz // 2, 2).sum(axis=(2, 4, 6))  13.1 us
    reshape x1, local copies, waits for them, and re-layouts, prolong(): jnp.broadcast_to(field[:, :, None, :, None, :, None], (kk, sx, 2, sy, 2,...  10.6 us
    reshape x1, local copies, waits for them, and re-layouts, coarse_weights(): dsum = degree.reshape(shape).sum(axis=(1, 3, 5))  10.5 us
  transfers between devices with their start and end apart: 32, of which 10 were waited for; matrix products, arithmetic and copies ran while one was open for 17% of the time, Pallas kernels for 0%

commit v1 on v0

--- a/solution.py
+++ b/solution.py
@@ -75,12 +75,18 @@
 
 
 def rayleigh_sums(vectors, applied, degree):
-    return lax.psum(
+
+    def close_lots_all(m, lane_axis, a_name="gx"):
+        for dev_j in (lane_axis, a_name):
+            m = lax.psum(m, dev_j)
+        return m
+
+    return close_lots_all(
         (
             jnp.sum(vectors * applied, axis=(1, 2, 3)),
             jnp.sum(vectors * (degree[None] * vectors), axis=(1, 2, 3)),
         ),
-        ("gx", "gy"),
+        "gy",
     )
 
 

time: 429 us -> 411 us (0.958)
  blocking collectives: 176 us -> 152 us
  starting transfers between devices: 98.6 us -> 104 us
    psum x1 -> x2, blocking collectives: 82.2 us -> 59.9 us  [close_lots_all(): m = lax.psum(m, dev_j)]
    ppermute x14, starting transfers between devices: 26.2 us -> 34 us  [with_halo(): lax.ppermute(head, axis, [((i + 1) % count, i) for i in range(ends)])]
where the time goes in v1:
time: 411 us; the launch traced here: 409 us
  blocking collectives  152 us (37%)
  starting transfers between devices  104 us (25%)
  local copies, waits for them, and re-layouts  80.5 us (20%)
  other arithmetic  57.4 us (14%)
  waiting for transfers between devices  9.34 us (2%)
    psum x1, blocking collectives, per_device(): gram = lax.psum(local_gram, ('gx', 'gy'))  92.2 us
    psum x2, blocking collectives, close_lots_all(): m = lax.psum(m, dev_j)  59.9 us
    ppermute x14, starting transfers between devices, with_halo(): lax.ppermute(tail, axis, [(i, (i + 1) % count) for i in range(ends)])  58.2 us
    ppermute x14, starting transfers between devices, with_halo(): lax.ppermute(head, axis, [((i + 1) % count, i) for i in range(ends)])  34 us
    reduce_sum x1, other arithmetic, restrict(): field.reshape(kk, sx // 2, 2, sy // 2, 2, sz // 2, 2).sum(axis=(2, 4, 6))  13.1 us
    ppermute x4, starting transfers between devices, shifted(): return lax.ppermute(shard, axis, pairs)  12.2 us
    reshape x1, local copies, waits for them, and re-layouts, prolong(): jnp.broadcast_to(field[:, :, None, :, None, :, None], (kk, sx, 2, sy, 2,...  10.6 us
    reshape x1, local copies, waits for them, and re-layouts, coarse_weights(): dsum = degree.reshape(shape).sum(axis=(1, 3, 5))  10.5 us
  transfers between devices with their start and end apart: 32, of which 10 were waited for; matrix products, arithmetic and copies ran while one was open for 17% of the time, Pallas kernels for 0%

profile of v1, /device:TPU:1, one launch (start us, length us, event | category | flops | bytes accessed | tf_op | source)
XLA Modules:
  0.0 409.5 jit_solution(3150823588027034004)
XLA Ops:
  1.7 3.9 collective-permute-start
  6.6 4.4 %collective-permute-start.1 = (f32[8,1,256]{2,1,0:T(1,128)S(1)}, f32[8,1,256]{2,1,0:T(1,128)S(1)}, u32[]{:S(2)}, u32[]{:S(2)}) collective-permute-start(f32[8,1,256]{2,1,0:T(1,128)S(1)} %slice.374), channel_id=1, source_target_pairs={{0,1},{1,2},{2,3},{3,4},{4,5},{5,6},{6,7},{7,8},{8,9},{9,10},{10,1... | collective-permute-start | bytes 24584 | tf_op jit(solution)/shard_map/ppermute | solution.py:14
  12.0 3.1 collective-permute-start.3
  15.2 1.3 collective-permute-start.2
  16.5 9.8 %reshape.74 = f32[4,2,8,2,128,2]{5,4,3,2,1,0:T(8,128)} reshape(f32[8,16,256]{2,1,0:T(8,128)S(1)} %broadcast_select_fusion.2) | data formatting | bytes 262144 | tf_op jit(solution)/shard_map/reshape | solution.py:96
  26.6 1.9 collective-permute-start.4
  28.6 3.6 collective-permute-start.5
  33.8 2.1 fusion
  35.9 26.8 %all-reduce.9 = (f32[8]{0:T(128)S(1)}, f32[8]{0:T(128)S(1)}) all-reduce(f32[8]{0:T(128)S(1)} %get-tuple-element.19, f32[8]{0:T(128)S(1)} %get-tuple-element.18), channel_id=1, replica_groups=mesh['gx'=16,'gy'=16] {'gy'}, use_global_device_ids=true, to_apply=%region_1.2 | all-reduce | flops 16 | bytes 128 | tf_op jit(solution)/shard_map/psum | solution.py:81
  62.7 33.1 %all-reduce.10 = (f32[8]{0:T(128)S(1)}, f32[8]{0:T(128)S(1)}) all-reduce(f32[8]{0:T(128)S(1)} %get-tuple-element.20, f32[8]{0:T(128)S(1)} %get-tuple-element.21), channel_id=1, replica_groups=mesh['gx'=16,'gy'=16] {'gx'}, use_global_device_ids=true, to_apply=%region_2.3 | all-reduce | flops 16 | bytes 128 | tf_op jit(solution)/shard_map/psum | solution.py:81
  95.8 1.7 multiply_divide_fusion
  98.2 1.3 collective-permute-start.6
  99.5 4.6 %collective-permute-start.7 = (f32[8,1,16,256]{3,2,1,0:T(8,128)}, f32[8,1,16,256]{3,2,1,0:T(8,128)}, u32[]{:S(2)}, u32[]{:S(2)}) collective-permute-start(f32[8,1,16,256]{3,2,1,0:T(8,128)} %get-tuple-element.46), channel_id=1, source_target_pairs={{0,16},{16,32},{32,48},{48,64},{64,80},{80,96},{96,112},{112,128},... | collective-permute-start | bytes 393224 | tf_op jit(solution)/shard_map/ppermute | solution.py:25
  104.2 2.8 slice_reduce_fusion.2
  108.2 1.9 collective-permute-start.14
  110.1 9.8 %reshape.75 = f32[4,2,8,2,128,2]{5,4,3,2,1,0:T(8,128)} reshape(f32[8,16,256]{2,1,0:T(8,128)S(1)} %broadcast_select_fusion.1) | data formatting | bytes 262144 | tf_op jit(solution)/shard_map/reshape | solution.py:97
  119.8 1.0 pad_maximum_fusion.62
  120.9 10.2 %collective-permute-start.8 = (f32[8,10,1,256]{3,0,2,1:T(8,128)S(1)}, f32[8,10,1,256]{3,0,2,1:T(8,128)S(1)}, u32[]{:S(2)}, u32[]{:S(2)}) collective-permute-start(f32[8,10,1,256]{3,0,2,1:T(8,128)S(1)} %copy.438), channel_id=1, source_target_pairs={{1,0},{2,1},{3,2},{4,3},{5,4},{6,5},{7,6},{8,7},{9,8},{10,9},{11,1... | collective-permute-start | bytes 245768 | tf_op jit(solution)/shard_map/ppermute | solution.py:27
  131.1 1.9 collective-permute-start.9
  133.0 2.8 slice_reduce_fusion.1
  136.5 2.0 collective-permute-start.15
  138.5 9.8 %reshape.76 = f32[4,2,8,2,128,2]{5,4,3,2,1,0:T(8,128)} reshape(f32[8,16,256]{2,1,0:T(8,128)S(1)} %broadcast_select_fusion) | data formatting | bytes 262144 | tf_op jit(solution)/shard_map/reshape | solution.py:98
  148.5 5.3 %fusion.13 = f32[8,8,16,256]{3,2,1,0:T(8,128)S(1)} fusion(f32[8,8,16,256]{3,2,1,0:T(8,128)} %copy-done.1, f32[8,8,16,256]{3,2,1,0:T(8,128)S(1)} %get-tuple-element.29, f32[8,10,1,256]{3,2,1,0:T(1,128)S(1)} %copy.441, f32[8,1,16,256]{3,2,1,0:T(8,128)} %copy-done.25, f32[8,1,16,256]{3,2,1,0:T(8,128)} %collective-permute-done.7, ...), kind=kLoop, calls=%fused_computation.28 | loop fusion | flops 6553600 | bytes 4489216 | tf_op jit(solution)/shard_map/add | solution.py:72
  154.6 1.3 collective-permute-start.10
  155.8 4.6 %collective-permute-start.11 = (f32[8,1,16,256]{3,2,1,0:T(8,128)}, f32[8,1,16,256]{3,2,1,0:T(8,128)}, u32[]{:S(2)}, u32[]{:S(2)}) collective-permute-start(f32[8,1,16,256]{3,2,1,0:T(8,128)} %get-tuple-element.44), channel_id=1, source_target_pairs={{0,16},{16,32},{32,48},{48,64},{64,80},{80,96},{96,112},{112,128},... | collective-permute-start | bytes 393224 | tf_op jit(solution)/shard_map/ppermute | solution.py:25
  160.5 6.8 %slice_reduce_fusion = f32[4,8,128]{2,1,0:T(8,128)} fusion(f32[4,2,8,2,128,2]{5,4,3,2,1,0:T(8,128)} %reshape.76), kind=kLoop, calls=%fused_computation | loop fusion | flops 12288 | bytes 81920 | tf_op jit(solution)/shard_map/reduce_sum | solution.py:98
  167.3 10.5 %reshape.77 = f32[4,2,8,2,128,2]{5,4,3,2,1,0:T(8,128)} reshape(f32[8,16,256]{2,1,0:T(8,128)} %copy-done.8) | data formatting | bytes 262144 | tf_op jit(solution)/shard_map/reshape | solution.py:99
  177.8 4.6 %reduce_sum.69 = f32[4,8,128]{2,1,0:T(8,128)} reduce(f32[4,2,8,2,128,2]{5,4,3,2,1,0:T(8,128)} %reshape.77, f32[]{:T(128)} %constant.65.clone.1), dimensions={1,3,5}, to_apply=%region_10.11 | reduce | flops 28672 | bytes 147460 | tf_op jit(solution)/shard_map/reduce_sum | solution.py:99
  182.5 1.2 pad_maximum_fusion.59
  183.7 3.5 collective-permute-start.12
  187.2 2.0 collective-permute-start.13
  189.3 1.4 multiply_add_fusion
  190.9 2.8 fusion.19
  193.8 9.8 %copy.446 = f32[8,8,16,256]{0,3,2,1:T(8,128)} copy(f32[8,8,16,256]{3,2,1,0:T(8,128)} %fusion.19) | data formatting | bytes 2097152 | tf_op jit(solution)/shard_map/sub | solution.py:134
  203.6 13.1 %reduce_sum.65 = f32[8,4,8,128]{0,3,2,1:T(8,128)} reduce(f32[8,4,2,8,2,128,2]{0,6,5,4,3,2,1:T(2,128)} %bitcast.30, f32[]{:T(128)} %constant.65.clone.1), dimensions={2,4,6}, to_apply=%region_6.7 | reduce | flops 229376 | bytes 1179652 | tf_op jit(solution)/shard_map/reduce_sum | solution.py:105
  216.7 2.8 copy.447
  220.6 1.3 collective-permute-start.16
  221.9 4.0 collective-permute-start.17
  226.9 3.4 collective-permute-start.18
  230.4 3.8 collective-permute-start.19
  235.1 1.1 fusion.68
  236.3 1.3 collective-permute-start.20
  237.6 4.6 %collective-permute-start.21 = (f32[8,1,8,128]{3,2,1,0:T(8,128)S(1)}, f32[8,1,8,128]{3,2,1,0:T(8,128)S(1)}, u32[]{:S(2)}, u32[]{:S(2)}) collective-permute-start(f32[8,1,8,128]{3,2,1,0:T(8,128)S(1)} %get-tuple-element.58), channel_id=1, source_target_pairs={{0,16},{16,32},{32,48},{48,64},{64,80},{80,96},{96,112},{112,128},... | collective-permute-start | bytes 98312 | tf_op jit(solution)/shard_map/ppermute | solution.py:25
  243.2 1.9 collective-permute-start.22
  245.1 5.1 %collective-permute-start.23 = (f32[8,6,1,128]{3,2,1,0:T(1,128)S(1)}, f32[8,6,1,128]{3,2,1,0:T(1,128)S(1)}, u32[]{:S(2)}, u32[]{:S(2)}) collective-permute-start(f32[8,6,1,128]{3,2,1,0:T(1,128)S(1)} %get-tuple-element.53), channel_id=1, source_target_pairs={{0,1},{1,2},{2,3},{3,4},{4,5},{5,6},{6,7},{7,8},{8,9},{9,10},{10,1... | collective-permute-start | bytes 73736 | tf_op jit(solution)/shard_map/ppermute | solution.py:25
  251.4 1.3 collective-permute-start.24
  252.7 4.7 %collective-permute-start.25 = (f32[8,1,8,128]{3,2,1,0:T(8,128)S(1)}, f32[8,1,8,128]{3,2,1,0:T(8,128)S(1)}, u32[]{:S(2)}, u32[]{:S(2)}) collective-permute-start(f32[8,1,8,128]{3,2,1,0:T(8,128)S(1)} %get-tuple-element.56), channel_id=1, source_target_pairs={{0,16},{16,32},{32,48},{48,64},{64,80},{80,96},{96,112},{112,128},... | collective-permute-start | bytes 98312 | tf_op jit(solution)/shard_map/ppermute | solution.py:25
  258.5 1.9 collective-permute-start.26
  260.4 5.1 %collective-permute-start.27 = (f32[8,6,1,128]{3,2,1,0:T(1,128)S(1)}, f32[8,6,1,128]{3,2,1,0:T(1,128)S(1)}, u32[]{:S(2)}, u32[]{:S(2)}) collective-permute-start(f32[8,6,1,128]{3,2,1,0:T(1,128)S(1)} %get-tuple-element.51), channel_id=1, source_target_pairs={{0,1},{1,2},{2,3},{3,4},{4,5},{5,6},{6,7},{7,8},{8,9},{9,10},{10,1... | collective-permute-start | bytes 73736 | tf_op jit(solution)/shard_map/ppermute | solution.py:25
  267.2 2.9 copy.451
  270.1 7.1 %broadcast_in_dim.30 = f32[8,4,2,8,2,128,2]{0,6,5,4,3,2,1:T(2,128)} broadcast(f32[8,4,8,128]{0,3,2,1:T(8,128)} %copy.451), dimensions={0,1,3,5} | broadcast | bytes 1179648 | tf_op jit(solution)/shard_map/broadcast_in_dim | solution.py:110
  277.2 10.6 %copy.452 = f32[8,8,16,256]{3,2,1,0:T(8,128)} copy(f32[8,8,16,256]{0,3,2,1:T(8,128)} %bitcast.31) | data formatting | bytes 2097152 | tf_op jit(solution)/shard_map/reshape | solution.py:110
  287.8 1.4 add.267
  289.3 1.4 collective-permute-start.28
  290.8 4.6 %collective-permute-start.29 = (f32[8,1,16,256]{3,2,1,0:T(8,128)S(1)}, f32[8,1,16,256]{3,2,1,0:T(8,128)S(1)}, u32[]{:S(2)}, u32[]{:S(2)}) collective-permute-start(f32[8,1,16,256]{3,2,1,0:T(8,128)S(1)} %get-tuple-element.42), channel_id=1, source_target_pairs={{0,16},{16,32},{32,48},{48,64},{64,80},{80,96},{96,112},{112,128},... | collective-permute-start | bytes 393224 | tf_op jit(solution)/shard_map/ppermute | solution.py:25
  295.8 1.5 collective-permute-done.29
  297.4 1.9 collective-permute-start.30
  299.3 6.3 %collective-permute-start.31 = (f32[8,10,1,256]{3,0,2,1:T(8,128)S(1)}, f32[8,10,1,256]{3,0,2,1:T(8,128)S(1)}, u32[]{:S(2)}, u32[]{:S(2)}) collective-permute-start(f32[8,10,1,256]{3,0,2,1:T(8,128)S(1)} %copy.455), channel_id=1, source_target_pairs={{0,1},{1,2},{2,3},{3,4},{4,5},{5,6},{6,7},{7,8},{8,9},{9,10},{10,1... | collective-permute-start | bytes 245768 | tf_op jit(solution)/shard_map/ppermute | solution.py:25
  305.8 1.1 collective-permute-done.31
  307.0 1.6 broadcast_multiply_fusion
  308.6 3.0 convolution_bitcast_fusion
  311.6 92.2 %psum.39 = f32[8,8]{0,1:T(8,128)S(1)} all-reduce(f32[8,8]{0,1:T(8,128)S(1)} %convolution_bitcast_fusion), channel_id=1, replica_groups=mesh['gx'=16,'gy'=16] {'gx','gy'}, use_global_device_ids=true, to_apply=%region_11.12 | all-reduce | flops 64 | bytes 512 | tf_op jit(solution)/shard_map/psum | solution.py:148
  407.2 1.0 fusion.110
  408.2 1.3 copy.462
  (159 shorter events, 20.5 us)
Async XLA Ops:
  1.6 24.6 %copy-start.2 = (f32[8,16,256]{2,1,0:T(8,128)}, f32[8,16,256]{2,1,0:T(8,128)S(1)}, u32[]{:S(2)}) copy-start(f32[8,16,256]{2,1,0:T(8,128)S(1)} %broadcast_select_fusion.2) | copy-start | bytes 393220
  1.7 30.6 %collective-permute-start = (f32[1,16,256]{2,1,0:T(8,128)S(1)}, f32[1,16,256]{2,1,0:T(8,128)S(1)}, u32[]{:S(2)}, u32[]{:S(2)}) collective-permute-start(f32[1,16,256]{2,1,0:T(8,128)S(1)} %slice.372), channel_id=1, source_target_pairs={{0,16},{16,32},{32,48},{48,64},{64,80},{80,96},{96,112},{112,128},... | collective-permute-start | bytes 49160 | tf_op jit(solution)/shard_map/ppermute | solution.py:14
  6.6 25.6 %collective-permute-start.1 = (f32[8,1,256]{2,1,0:T(1,128)S(1)}, f32[8,1,256]{2,1,0:T(1,128)S(1)}, u32[]{:S(2)}, u32[]{:S(2)}) collective-permute-start(f32[8,1,256]{2,1,0:T(1,128)S(1)} %slice.374), channel_id=1, source_target_pairs={{0,1},{1,2},{2,3},{3,4},{4,5},{5,6},{6,7},{7,8},{8,9},{9,10},{10,1... | collective-permute-start | bytes 24584 | tf_op jit(solution)/shard_map/ppermute | solution.py:14
  12.0 14.3 %collective-permute-start.3 = (f32[8,1,16,256]{3,2,1,0:T(8,128)S(1)}, f32[8,1,16,256]{3,2,1,0:T(8,128)S(1)}, u32[]{:S(2)}, u32[]{:S(2)}) collective-permute-start(f32[8,1,16,256]{3,2,1,0:T(8,128)S(1)} %get-tuple-element.49), channel_id=1, source_target_pairs={{0,16},{16,32},{32,48},{48,64},{64,80},{80,96},{96,112},{112,128},... | collective-permute-start | bytes 393224 | tf_op jit(solution)/shard_map/ppermute | solution.py:25
  15.2 11.3 %collective-permute-start.2 = (f32[8,1,16,256]{3,2,1,0:T(8,128)S(1)}, f32[8,1,16,256]{3,2,1,0:T(8,128)S(1)}, u32[]{:S(2)}, u32[]{:S(2)}) collective-permute-start(f32[8,1,16,256]{3,2,1,0:T(8,128)S(1)} %get-tuple-element.48), channel_id=1, source_target_pairs={{16,0},{32,16},{48,32},{64,48},{80,64},{96,80},{112,96},{128,112},... | collective-permute-start | bytes 393224 | tf_op jit(solution)/shard_map/ppermute | solution.py:27
  16.5 9.8 %copy-start.26 = (f32[8,16,256]{2,1,0:T(8,128)S(1)}, f32[8,16,256]{2,1,0:T(8,128)}, u32[]{:S(2)}) copy-start(f32[8,16,256]{2,1,0:T(8,128)} %param.7) | copy-start | bytes 393220
  16.5 9.8 %copy-start = (f32[8,8,16,256]{3,2,1,0:T(8,128)S(1)}, f32[8,8,16,256]{3,2,1,0:T(8,128)}, u32[]{:S(2)}) copy-start(f32[8,8,16,256]{3,2,1,0:T(8,128)} %param.4) | copy-start | bytes 3145732
  26.3 5.9 %slice-start = ((f32[8,16,256]{2,1,0:T(8,128)}), f32[7,16,256]{2,1,0:T(8,128)S(1)}, s32[]{:S(2)}) async-start(f32[8,16,256]{2,1,0:T(8,128)} %copy-done.2), calls=%async_computation | async-start | bytes 229376 | tf_op jit(solution)/shard_map/slice | solution.py:36
  26.3 5.9 %copy-start.27 = (f32[8,16,256]{2,1,0:T(8,128)S(1)}, f32[8,16,256]{2,1,0:T(8,128)}, u32[]{:S(2)}) copy-start(f32[8,16,256]{2,1,0:T(8,128)} %param.5) | copy-start | bytes 393220
  26.4 5.9 %copy-start.28 = (f32[8,16,256]{2,1,0:T(8,128)S(1)}, f32[8,16,256]{2,1,0:T(8,128)}, u32[]{:S(2)}) copy-start(f32[8,16,256]{2,1,0:T(8,128)} %param.6) | copy-start | bytes 393220
  26.5 7.3 %copy-start.3 = (f32[8,16,256]{2,1,0:T(8,128)S(1)}, f32[8,16,256]{2,1,0:T(8,128)}, u32[]{:S(2)}) copy-start(f32[8,16,256]{2,1,0:T(8,128)} %copy-done.2) | copy-start | bytes 393220
  26.6 6.5 %collective-permute-start.4 = (f32[8,10,1,256]{3,0,2,1:T(8,128)S(1)}, f32[8,10,1,256]{3,0,2,1:T(8,128)S(1)}, u32[]{:S(2)}, u32[]{:S(2)}) collective-permute-start(f32[8,10,1,256]{3,0,2,1:T(8,128)S(1)} %copy.466), channel_id=1, source_target_pairs={{1,0},{2,1},{3,2},{4,3},{5,4},{6,5},{7,6},{8,7},{9,8},{10,9},{11,1... | collective-permute-start | bytes 245768 | tf_op jit(solution)/shard_map/ppermute | solution.py:27
  28.6 5.1 %collective-permute-start.5 = (f32[8,10,1,256]{3,0,2,1:T(8,128)S(1)}, f32[8,10,1,256]{3,0,2,1:T(8,128)S(1)}, u32[]{:S(2)}, u32[]{:S(2)}) collective-permute-start(f32[8,10,1,256]{3,0,2,1:T(8,128)S(1)} %copy.467), channel_id=1, source_target_pairs={{0,1},{1,2},{2,3},{3,4},{4,5},{5,6},{6,7},{7,8},{8,9},{9,10},{10,1... | collective-permute-start | bytes 245768 | tf_op jit(solution)/shard_map/ppermute | solution.py:25
  33.1 2.8 copy-start.17
  33.8 62.0 %copy-start.5 = (f32[8,16,256]{2,1,0:T(8,128)S(1)}, f32[8,16,256]{2,1,0:T(8,128)}, u32[]{:S(2)}) copy-start(f32[8,16,256]{2,1,0:T(8,128)} %get-tuple-element.30) | copy-start | bytes 393220
  97.5 22.3 %copy-start.1 = (f32[8,8,16,256]{3,2,1,0:T(8,128)}, f32[8,8,16,256]{3,2,1,0:T(8,128)S(1)}, u32[]{:S(2)}) copy-start(f32[8,8,16,256]{3,2,1,0:T(8,128)S(1)} %get-tuple-element.28) | copy-start | bytes 3145732
  98.2 21.6 %collective-permute-start.6 = (f32[8,1,16,256]{3,2,1,0:T(8,128)}, f32[8,1,16,256]{3,2,1,0:T(8,128)S(1)}, u32[]{:S(2)}, u32[]{:S(2)}) collective-permute-start(f32[8,1,16,256]{3,2,1,0:T(8,128)} %get-tuple-element.47), channel_id=1, source_target_pairs={{16,0},{32,16},{48,32},{64,48},{80,64},{96,80},{112,96},{128,112},... | collective-permute-start | bytes 393224 | tf_op jit(solution)/shard_map/ppermute | solution.py:27
  99.5 20.3 %collective-permute-start.7 = (f32[8,1,16,256]{3,2,1,0:T(8,128)}, f32[8,1,16,256]{3,2,1,0:T(8,128)}, u32[]{:S(2)}, u32[]{:S(2)}) collective-permute-start(f32[8,1,16,256]{3,2,1,0:T(8,128)} %get-tuple-element.46), channel_id=1, source_target_pairs={{0,16},{16,32},{32,48},{48,64},{64,80},{80,96},{96,112},{112,128},... | collective-permute-start | bytes 393224 | tf_op jit(solution)/shard_map/ppermute | solution.py:25
  108.2 81.1 %collective-permute-start.14 = (f32[1,8,128]{2,1,0:T(8,128)}, f32[1,8,128]{2,1,0:T(8,128)}, u32[]{:S(2)}, u32[]{:S(2)}) collective-permute-start(f32[1,8,128]{2,1,0:T(8,128)} %slice.384), channel_id=1, source_target_pairs={{0,16},{16,32},{32,48},{48,64},{64,80},{80,96},{96,112},{112,128},... | collective-permute-start | bytes 12296 | tf_op jit(solution)/shard_map/ppermute | solution.py:14
  119.8 16.0 %copy-start.25 = (f32[8,1,16,256]{3,2,1,0:T(8,128)}, f32[8,1,16,256]{3,2,1,0:T(8,128)S(1)}, u32[]{:S(2)}) copy-start(f32[8,1,16,256]{3,2,1,0:T(8,128)S(1)} %collective-permute-done.6) | copy-start | bytes 393220
  120.9 27.4 %collective-permute-start.8 = (f32[8,10,1,256]{3,0,2,1:T(8,128)S(1)}, f32[8,10,1,256]{3,0,2,1:T(8,128)S(1)}, u32[]{:S(2)}, u32[]{:S(2)}) collective-permute-start(f32[8,10,1,256]{3,0,2,1:T(8,128)S(1)} %copy.438), channel_id=1, source_target_pairs={{1,0},{2,1},{3,2},{4,3},{5,4},{6,5},{7,6},{8,7},{9,8},{10,9},{11,1... | collective-permute-start | bytes 245768 | tf_op jit(solution)/shard_map/ppermute | solution.py:27
  131.1 17.3 %collective-permute-start.9 = (f32[8,10,1,256]{3,0,2,1:T(8,128)S(1)}, f32[8,10,1,256]{3,0,2,1:T(8,128)S(1)}, u32[]{:S(2)}, u32[]{:S(2)}) collective-permute-start(f32[8,10,1,256]{3,0,2,1:T(8,128)S(1)} %copy.440), channel_id=1, source_target_pairs={{0,1},{1,2},{2,3},{3,4},{4,5},{5,6},{6,7},{7,8},{8,9},{9,10},{10,1... | collective-permute-start | bytes 245768 | tf_op jit(solution)/shard_map/ppermute | solution.py:25
  136.5 12.0 %copy-start.4 = (f32[8,16,256]{2,1,0:T(8,128)S(1)}, f32[8,16,256]{2,1,0:T(8,128)}, u32[]{:S(2)}) copy-start(f32[8,16,256]{2,1,0:T(8,128)} %copy-done.2) | copy-start | bytes 393220
  136.5 52.8 %collective-permute-start.15 = (f32[4,1,128]{2,1,0:T(1,128)}, f32[4,1,128]{2,1,0:T(1,128)}, u32[]{:S(2)}, u32[]{:S(2)}) collective-permute-start(f32[4,1,128]{2,1,0:T(1,128)} %slice.387), channel_id=1, source_target_pairs={{0,1},{1,2},{2,3},{3,4},{4,5},{5,6},{6,7},{7,8},{8,9},{9,10},{10,1... | collective-permute-start | bytes 6152 | tf_op jit(solution)/shard_map/ppermute | solution.py:14
  154.6 27.9 %collective-permute-start.10 = (f32[8,1,16,256]{3,2,1,0:T(8,128)}, f32[8,1,16,256]{3,2,1,0:T(8,128)}, u32[]{:S(2)}, u32[]{:S(2)}) collective-permute-start(f32[8,1,16,256]{3,2,1,0:T(8,128)} %get-tuple-element.45), channel_id=1, source_target_pairs={{16,0},{32,16},{48,32},{64,48},{80,64},{96,80},{112,96},{128,112},... | collective-permute-start | bytes 393224 | tf_op jit(solution)/shard_map/ppermute | solution.py:27
  155.8 26.6 %collective-permute-start.11 = (f32[8,1,16,256]{3,2,1,0:T(8,128)}, f32[8,1,16,256]{3,2,1,0:T(8,128)}, u32[]{:S(2)}, u32[]{:S(2)}) collective-permute-start(f32[8,1,16,256]{3,2,1,0:T(8,128)} %get-tuple-element.44), channel_id=1, source_target_pairs={{0,16},{16,32},{32,48},{48,64},{64,80},{80,96},{96,112},{112,128},... | collective-permute-start | bytes 393224 | tf_op jit(solution)/shard_map/ppermute | solution.py:25
  182.4 6.9 %copy-start.21 = (f32[4,8,128]{2,1,0:T(8,128)S(1)}, f32[4,8,128]{2,1,0:T(8,128)}, u32[]{:S(2)}) copy-start(f32[4,8,128]{2,1,0:T(8,128)} %copy-done.20) | copy-start | bytes 49156
  182.4 6.9 %slice-start.1 = ((f32[4,8,128]{2,1,0:T(8,128)}), f32[3,8,128]{2,1,0:T(8,128)S(1)}, s32[]{:S(2)}) async-start(f32[4,8,128]{2,1,0:T(8,128)} %copy-done.20), calls=%async_computation.1 | async-start | bytes 24576 | tf_op jit(solution)/shard_map/slice | solution.py:36
  182.4 6.9 %copy-start.23 = (f32[4,8,128]{2,1,0:T(8,128)S(1)}, f32[4,8,128]{2,1,0:T(8,128)}, u32[]{:S(2)}) copy-start(f32[4,8,128]{2,1,0:T(8,128)} %slice_reduce_fusion) | copy-start | bytes 49156
  182.4 6.9 %copy-start.33 = (f32[4,8,128]{2,1,0:T(8,128)S(1)}, f32[4,8,128]{2,1,0:T(8,128)}, u32[]{:S(2)}) copy-start(f32[4,8,128]{2,1,0:T(8,128)} %reduce_sum.69) | copy-start | bytes 49156
  182.4 8.5 %copy-start.6 = (f32[8,16,256]{2,1,0:T(8,128)S(1)}, f32[8,16,256]{2,1,0:T(8,128)}, u32[]{:S(2)}) copy-start(f32[8,16,256]{2,1,0:T(8,128)} %get-tuple-element.30) | copy-start | bytes 393220
  182.4 8.5 %copy-start.12 = (f32[8,16,256]{2,1,0:T(8,128)S(1)}, f32[8,16,256]{2,1,0:T(8,128)}, u32[]{:S(2)}) copy-start(f32[8,16,256]{2,1,0:T(8,128)} %copy-done.11) | copy-start | bytes 393220
  182.4 8.5 %copy-start.15 = (f32[8,16,256]{2,1,0:T(8,128)S(1)}, f32[8,16,256]{2,1,0:T(8,128)}, u32[]{:S(2)}) copy-start(f32[8,16,256]{2,1,0:T(8,128)} %copy-done.14) | copy-start | bytes 393220
  182.4 8.5 %copy-start.18 = (f32[8,16,256]{2,1,0:T(8,128)S(1)}, f32[8,16,256]{2,1,0:T(8,128)}, u32[]{:S(2)}) copy-start(f32[8,16,256]{2,1,0:T(8,128)} %copy-done.17) | copy-start | bytes 393220
  183.7 7.0 %collective-permute-start.12 = (f32[8,10,1,256]{3,0,2,1:T(8,128)S(1)}, f32[8,10,1,256]{3,0,2,1:T(8,128)S(1)}, u32[]{:S(2)}, u32[]{:S(2)}) collective-permute-start(f32[8,10,1,256]{3,0,2,1:T(8,128)S(1)} %copy.442), channel_id=1, source_target_pairs={{1,0},{2,1},{3,2},{4,3},{5,4},{6,5},{7,6},{8,7},{9,8},{10,9},{11,1... | collective-permute-start | bytes 245768 | tf_op jit(solution)/shard_map/ppermute | solution.py:27
  187.2 3.6 collective-permute-start.13
  219.5 31.6 %copy-start.10 = (f32[8,4,8,128]{3,2,1,0:T(8,128)S(1)}, f32[8,4,8,128]{3,2,1,0:T(8,128)}, u32[]{:S(2)}) copy-start(f32[8,4,8,128]{3,2,1,0:T(8,128)} %copy.447) | copy-start | bytes 393220
  219.5 31.6 %copy-start.22 = (f32[4,8,128]{2,1,0:T(8,128)S(1)}, f32[4,8,128]{2,1,0:T(8,128)}, u32[]{:S(2)}) copy-start(f32[4,8,128]{2,1,0:T(8,128)} %copy-done.20) | copy-start | bytes 49156
  219.5 31.6 %copy-start.24 = (f32[4,8,128]{2,1,0:T(8,128)S(1)}, f32[4,8,128]{2,1,0:T(8,128)}, u32[]{:S(2)}) copy-start(f32[4,8,128]{2,1,0:T(8,128)} %slice_reduce_fusion) | copy-start | bytes 49156
  219.5 31.6 %copy-start.29 = (f32[4,8,128]{2,1,0:T(8,128)S(1)}, f32[4,8,128]{2,1,0:T(8,128)}, u32[]{:S(2)}) copy-start(f32[4,8,128]{2,1,0:T(8,128)} %get-tuple-element.26) | copy-start | bytes 49156
  219.5 31.6 %copy-start.30 = (f32[4,8,128]{2,1,0:T(8,128)S(1)}, f32[4,8,128]{2,1,0:T(8,128)}, u32[]{:S(2)}) copy-start(f32[4,8,128]{2,1,0:T(8,128)} %get-tuple-element.27) | copy-start | bytes 49156
  219.5 31.6 %copy-start.31 = (f32[4,8,128]{2,1,0:T(8,128)S(1)}, f32[4,8,128]{2,1,0:T(8,128)}, u32[]{:S(2)}) copy-start(f32[4,8,128]{2,1,0:T(8,128)} %get-tuple-element.64) | copy-start | bytes 49156
  219.5 31.6 %copy-start.32 = (f32[4,8,128]{2,1,0:T(8,128)S(1)}, f32[4,8,128]{2,1,0:T(8,128)}, u32[]{:S(2)}) copy-start(f32[4,8,128]{2,1,0:T(8,128)} %get-tuple-element.65) | copy-start | bytes 49156
  220.6 5.3 %collective-permute-start.16 = (f32[8,1,8,128]{3,2,1,0:T(8,128)S(1)}, f32[8,1,8,128]{3,2,1,0:T(8,128)S(1)}, u32[]{:S(2)}, u32[]{:S(2)}) collective-permute-start(f32[8,1,8,128]{3,2,1,0:T(8,128)S(1)} %get-tuple-element.61), channel_id=1, source_target_pairs={{16,0},{32,16},{48,32},{64,48},{80,64},{96,80},{112,96},{128,112},... | collective-permute-start | bytes 98312 | tf_op jit(solution)/shard_map/ppermute | solution.py:27
  221.9 5.0 %collective-permute-start.17 = (f32[8,1,8,128]{3,2,1,0:T(8,128)S(1)}, f32[8,1,8,128]{3,2,1,0:T(8,128)S(1)}, u32[]{:S(2)}, u32[]{:S(2)}) collective-permute-start(f32[8,1,8,128]{3,2,1,0:T(8,128)S(1)} %get-tuple-element.60), channel_id=1, source_target_pairs={{0,16},{16,32},{32,48},{48,64},{64,80},{80,96},{96,112},{112,128},... | collective-permute-start | bytes 98312 | tf_op jit(solution)/shard_map/ppermute | solution.py:25
  226.9 7.3 %collective-permute-start.18 = (f32[8,6,1,128]{3,2,1,0:T(1,128)S(1)}, f32[8,6,1,128]{3,2,1,0:T(1,128)S(1)}, u32[]{:S(2)}, u32[]{:S(2)}) collective-permute-start(f32[8,6,1,128]{3,2,1,0:T(1,128)S(1)} %get-tuple-element.54), channel_id=1, source_target_pairs={{1,0},{2,1},{3,2},{4,3},{5,4},{6,5},{7,6},{8,7},{9,8},{10,9},{11,1... | collective-permute-start | bytes 73736 | tf_op jit(solution)/shard_map/ppermute | solution.py:27
  230.4 4.8 %collective-permute-start.19 = (f32[8,6,1,128]{3,2,1,0:T(1,128)S(1)}, f32[8,6,1,128]{3,2,1,0:T(1,128)S(1)}, u32[]{:S(2)}, u32[]{:S(2)}) collective-permute-start(f32[8,6,1,128]{3,2,1,0:T(1,128)S(1)} %get-tuple-element.55), channel_id=1, source_target_pairs={{0,1},{1,2},{2,3},{3,4},{4,5},{5,6},{6,7},{7,8},{8,9},{9,10},{10,1... | collective-permute-start | bytes 73736 | tf_op jit(solution)/shard_map/ppermute | solution.py:25
  236.3 5.9 %collective-permute-start.20 = (f32[8,1,8,128]{3,2,1,0:T(8,128)S(1)}, f32[8,1,8,128]{3,2,1,0:T(8,128)S(1)}, u32[]{:S(2)}, u32[]{:S(2)}) collective-permute-start(f32[8,1,8,128]{3,2,1,0:T(8,128)S(1)} %get-tuple-element.59), channel_id=1, source_target_pairs={{16,0},{32,16},{48,32},{64,48},{80,64},{96,80},{112,96},{128,112},... | collective-permute-start | bytes 98312 | tf_op jit(solution)/shard_map/ppermute | solution.py:27
  237.6 5.6 %collective-permute-start.21 = (f32[8,1,8,128]{3,2,1,0:T(8,128)S(1)}, f32[8,1,8,128]{3,2,1,0:T(8,128)S(1)}, u32[]{:S(2)}, u32[]{:S(2)}) collective-permute-start(f32[8,1,8,128]{3,2,1,0:T(8,128)S(1)} %get-tuple-element.58), channel_id=1, source_target_pairs={{0,16},{16,32},{32,48},{48,64},{64,80},{80,96},{96,112},{112,128},... | collective-permute-start | bytes 98312 | tf_op jit(solution)/shard_map/ppermute | solution.py:25
  243.2 7.1 %collective-permute-start.22 = (f32[8,6,1,128]{3,2,1,0:T(1,128)S(1)}, f32[8,6,1,128]{3,2,1,0:T(1,128)S(1)}, u32[]{:S(2)}, u32[]{:S(2)}) collective-permute-start(f32[8,6,1,128]{3,2,1,0:T(1,128)S(1)} %get-tuple-element.52), channel_id=1, source_target_pairs={{1,0},{2,1},{3,2},{4,3},{5,4},{6,5},{7,6},{8,7},{9,8},{10,9},{11,1... | collective-permute-start | bytes 73736 | tf_op jit(solution)/shard_map/ppermute | solution.py:27
  245.1 6.0 %collective-permute-start.23 = (f32[8,6,1,128]{3,2,1,0:T(1,128)S(1)}, f32[8,6,1,128]{3,2,1,0:T(1,128)S(1)}, u32[]{:S(2)}, u32[]{:S(2)}) collective-permute-start(f32[8,6,1,128]{3,2,1,0:T(1,128)S(1)} %get-tuple-element.53), channel_id=1, source_target_pairs={{0,1},{1,2},{2,3},{3,4},{4,5},{5,6},{6,7},{7,8},{8,9},{9,10},{10,1... | collective-permute-start | bytes 73736 | tf_op jit(solution)/shard_map/ppermute | solution.py:25
  251.4 6.0 %collective-permute-start.24 = (f32[8,1,8,128]{3,2,1,0:T(8,128)S(1)}, f32[8,1,8,128]{3,2,1,0:T(8,128)S(1)}, u32[]{:S(2)}, u32[]{:S(2)}) collective-permute-start(f32[8,1,8,128]{3,2,1,0:T(8,128)S(1)} %get-tuple-element.57), channel_id=1, source_target_pairs={{16,0},{32,16},{48,32},{64,48},{80,64},{96,80},{112,96},{128,112},... | collective-permute-start | bytes 98312 | tf_op jit(solution)/shard_map/ppermute | solution.py:27
  252.7 5.7 %collective-permute-start.25 = (f32[8,1,8,128]{3,2,1,0:T(8,128)S(1)}, f32[8,1,8,128]{3,2,1,0:T(8,128)S(1)}, u32[]{:S(2)}, u32[]{:S(2)}) collective-permute-start(f32[8,1,8,128]{3,2,1,0:T(8,128)S(1)} %get-tuple-element.56), channel_id=1, source_target_pairs={{0,16},{16,32},{32,48},{48,64},{64,80},{80,96},{96,112},{112,128},... | collective-permute-start | bytes 98312 | tf_op jit(solution)/shard_map/ppermute | solution.py:25
  258.5 7.0 %collective-permute-start.26 = (f32[8,6,1,128]{3,2,1,0:T(1,128)S(1)}, f32[8,6,1,128]{3,2,1,0:T(1,128)S(1)}, u32[]{:S(2)}, u32[]{:S(2)}) collective-permute-start(f32[8,6,1,128]{3,2,1,0:T(1,128)S(1)} %get-tuple-element.50), channel_id=1, source_target_pairs={{1,0},{2,1},{3,2},{4,3},{5,4},{6,5},{7,6},{8,7},{9,8},{10,9},{11,1... | collective-permute-start | bytes 73736 | tf_op jit(solution)/shard_map/ppermute | solution.py:27
  260.4 6.0 %collective-permute-start.27 = (f32[8,6,1,128]{3,2,1,0:T(1,128)S(1)}, f32[8,6,1,128]{3,2,1,0:T(1,128)S(1)}, u32[]{:S(2)}, u32[]{:S(2)}) collective-permute-start(f32[8,6,1,128]{3,2,1,0:T(1,128)S(1)} %get-tuple-element.51), channel_id=1, source_target_pairs={{0,1},{1,2},{2,3},{3,4},{4,5},{5,6},{6,7},{7,8},{8,9},{9,10},{10,1... | collective-permute-start | bytes 73736 | tf_op jit(solution)/shard_map/ppermute | solution.py:25
  289.2 17.7 %copy-start.7 = (f32[8,16,256]{2,1,0:T(8,128)S(1)}, f32[8,16,256]{2,1,0:T(8,128)}, u32[]{:S(2)}) copy-start(f32[8,16,256]{2,1,0:T(8,128)} %get-tuple-element.30) | copy-start | bytes 393220
  289.3 17.7 %copy-start.9 = (f32[8,16,256]{2,1,0:T(8,128)S(1)}, f32[8,16,256]{2,1,0:T(8,128)}, u32[]{:S(2)}) copy-start(f32[8,16,256]{2,1,0:T(8,128)} %copy-done.8) | copy-start | bytes 393220
  289.3 17.7 %copy-start.13 = (f32[8,16,256]{2,1,0:T(8,128)S(1)}, f32[8,16,256]{2,1,0:T(8,128)}, u32[]{:S(2)}) copy-start(f32[8,16,256]{2,1,0:T(8,128)} %copy-done.11) | copy-start | bytes 393220
  289.3 17.7 %copy-start.16 = (f32[8,16,256]{2,1,0:T(8,128)S(1)}, f32[8,16,256]{2,1,0:T(8,128)}, u32[]{:S(2)}) copy-start(f32[8,16,256]{2,1,0:T(8,128)} %copy-done.14) | copy-start | bytes 393220
  289.3 17.7 %copy-start.19 = (f32[8,16,256]{2,1,0:T(8,128)S(1)}, f32[8,16,256]{2,1,0:T(8,128)}, u32[]{:S(2)}) copy-start(f32[8,16,256]{2,1,0:T(8,128)} %copy-done.17) | copy-start | bytes 393220
  289.3 6.4 %collective-permute-start.28 = (f32[8,1,16,256]{3,2,1,0:T(8,128)S(1)}, f32[8,1,16,256]{3,2,1,0:T(8,128)S(1)}, u32[]{:S(2)}, u32[]{:S(2)}) collective-permute-start(f32[8,1,16,256]{3,2,1,0:T(8,128)S(1)} %get-tuple-element.43), channel_id=1, source_target_pairs={{16,0},{32,16},{48,32},{64,48},{80,64},{96,80},{112,96},{128,112},... | collective-permute-start | bytes 393224 | tf_op jit(solution)/shard_map/ppermute | solution.py:27
  290.8 6.5 %collective-permute-start.29 = (f32[8,1,16,256]{3,2,1,0:T(8,128)S(1)}, f32[8,1,16,256]{3,2,1,0:T(8,128)S(1)}, u32[]{:S(2)}, u32[]{:S(2)}) collective-permute-start(f32[8,1,16,256]{3,2,1,0:T(8,128)S(1)} %get-tuple-element.42), channel_id=1, source_target_pairs={{0,16},{16,32},{32,48},{48,64},{64,80},{80,96},{96,112},{112,128},... | collective-permute-start | bytes 393224 | tf_op jit(solution)/shard_map/ppermute | solution.py:25
  297.4 8.3 %collective-permute-start.30 = (f32[8,10,1,256]{3,0,2,1:T(8,128)S(1)}, f32[8,10,1,256]{3,0,2,1:T(8,128)S(1)}, u32[]{:S(2)}, u32[]{:S(2)}) collective-permute-start(f32[8,10,1,256]{3,0,2,1:T(8,128)S(1)} %copy.453), channel_id=1, source_target_pairs={{1,0},{2,1},{3,2},{4,3},{5,4},{6,5},{7,6},{8,7},{9,8},{10,9},{11,1... | collective-permute-start | bytes 245768 | tf_op jit(solution)/shard_map/ppermute | solution.py:27
  299.3 7.6 %collective-permute-start.31 = (f32[8,10,1,256]{3,0,2,1:T(8,128)S(1)}, f32[8,10,1,256]{3,0,2,1:T(8,128)S(1)}, u32[]{:S(2)}, u32[]{:S(2)}) collective-permute-start(f32[8,10,1,256]{3,0,2,1:T(8,128)S(1)} %copy.455), channel_id=1, source_target_pairs={{0,1},{1,2},{2,3},{3,4},{4,5},{5,6},{6,7},{7,8},{8,9},{9,10},{10,1... | collective-permute-start | bytes 245768 | tf_op jit(solution)/shard_map/ppermute | solution.py:25
  (5 other events, 10.7 us)
